TPU v7x, 32 devices: a whole 2x2x4 slice. The times are simulated.
32 devices in a mesh: ctx: 16 (over z, y, x), kvh: 2 (over core).
Axes of the slice: x: 2, y: 2, z: 4, core: 2. Of those that a mesh axis runs over, the one named last changes fastest.
Arguments:
- queries: bfloat16 [2, 4096, 1024], P('kvh', 'ctx'), may hold values from -30 to 30
- keys: bfloat16 [2, 4096, 128], P('kvh', 'ctx'), may hold values from -12 to 12
- values: bfloat16 [2, 4096, 128], P('kvh', 'ctx'), may hold values from -6 to 6
- doc_lengths: int32 [8], replicated, may hold values from 1 to 2048, 4096 in all
- w_out: bfloat16 [2048, 8192], P('kvh'), may hold values from -0.125 to 0.125
Outputs:
- layer_out: bfloat16 [4096, 8192], P(('ctx', 'kvh'))
Inputs may be any that keep to these rules, and one draw needn't show every extreme that they name: `doc_lengths`: the lengths sum to 4096; the longest is exactly 2048.
All inputs are finite; a program needn't handle non-finite values.
Results may differ from a plain program's by a relative error of at most 0.013.
Values may be sent and summed in bfloat16 or wider, within the bound.
A program may use at most 192 MiB of HBM per device.

v0:
```python
import jax
import jax.numpy as jnp
from jax import lax
from jax.sharding import PartitionSpec as P

NEG = -1e30


def on_device(queries, keys, values, doc_lengths, w_out):
    ctx_count = lax.axis_size("ctx")
    device = lax.axis_index("ctx")
    head_width = keys.shape[2]
    block_rows = keys.shape[1] // 2
    groups = queries.shape[2] // head_width
    score_scale = head_width ** (-0.5)
    query_heads = queries[0].reshape(2, block_rows, groups, head_width)
    offsets = jnp.arange(block_rows, dtype=jnp.int32)
    own_places = jnp.stack([device, 2 * ctx_count - 1 - device])
    query_pos = own_places[:, None] * block_rows + offsets[None, :]
    doc_ends = jnp.cumsum(doc_lengths)
    doc_start = jnp.sum(
        doc_lengths[None, None, :]
        * (doc_ends[None, None, :] <= query_pos[:, :, None]).astype(jnp.int32),
        axis=2,
    )

    def update(carry, slot_queries, slot_pos, slot_start, key_tile, value_tile, key_pos):
        allowed = (key_pos[:, None, :] <= slot_pos[:, :, None]) & (
            key_pos[:, None, :] >= slot_start[:, :, None]
        )

        def absorb(state):
            running_max, denominator, summed = state
            scores = (
                jnp.einsum(
                    "sihd,jd->shij", slot_queries, key_tile[0], preferred_element_type=jnp.float32
                )
                * score_scale
            )
            scores = jnp.where(allowed[:, None], scores, NEG)
            new_max = jnp.maximum(running_max, jnp.max(scores, axis=3))
            weights = jnp.where(allowed[:, None], jnp.exp(scores - new_max[..., None]), 0.0)
            rescale = jnp.exp(running_max - new_max)
            denominator = denominator * rescale + jnp.sum(weights, axis=3)
            contrib = jnp.einsum(
                "shij,jd->sihd",
                weights.astype(jnp.bfloat16),
                value_tile[0],
                preferred_element_type=jnp.float32,
            )
            summed = summed * jnp.transpose(rescale, (0, 2, 1))[..., None] + contrib
            return (new_max, denominator, summed)

        return lax.cond(jnp.any(allowed) & True, absorb, lambda state: state, carry)

    initial = (
        jnp.full((2, groups, block_rows), NEG, jnp.float32),
        jnp.zeros((2, groups, block_rows), jnp.float32),
        jnp.zeros((2, block_rows, groups, head_width), jnp.float32),
    )
    key_piece = lax.all_gather(keys, "ctx", axis=1, tiled=True)
    value_piece = lax.all_gather(values, "ctx", axis=1, tiled=True)
    shard_rows = 2 * block_rows
    shard_count = key_piece.shape[1] // shard_rows
    limit = max(1024, shard_rows)
    per_step = 1
    for divisor in range(1, shard_count + 1):
        if shard_count % divisor == 0 and divisor * shard_rows <= limit:
            per_step = divisor
    tile_rows = per_step * shard_rows
    tile_offsets = jnp.arange(tile_rows, dtype=jnp.int32)

    def absorb_tile(tile_number, state):
        start = (tile_number * tile_rows).astype(jnp.int32)
        key_tile = lax.dynamic_slice_in_dim(key_piece[0], start, tile_rows, 0)
        value_tile = lax.dynamic_slice_in_dim(value_piece[0], start, tile_rows, 0)
        global_row = start + tile_offsets
        global_block = global_row // block_rows
        holder = global_block // 2
        block_place = jnp.where(global_block % 2 == 0, holder, 2 * ctx_count - 1 - holder)
        key_pos = block_place * block_rows + global_row % block_rows
        return update(
            state,
            query_heads,
            query_pos,
            doc_start,
            key_tile[None],
            value_tile[None],
            key_pos[None],
        )

    state = lax.fori_loop(0, shard_count // per_step, absorb_tile, initial)
    running_max, denominator, summed = state
    attended = summed / jnp.transpose(denominator, (0, 2, 1))[..., None]
    attended = attended.astype(jnp.bfloat16).reshape(2 * block_rows, groups * head_width)
    return lax.psum_scatter(
        jnp.dot(attended, w_out, preferred_element_type=jnp.float32).astype(jnp.bfloat16),
        "kvh",
        scatter_dimension=0,
        tiled=True,
    )


def solution(mesh):
    in_specs = (
        P("kvh", "ctx", None),
        P("kvh", "ctx", None),
        P("kvh", "ctx", None),
        P(),
        P("kvh", None),
    )
    out_specs = P(("ctx", "kvh"), None)
    return jax.shard_map(
        on_device, mesh=mesh, in_specs=in_specs, out_specs=out_specs, check_vma=False
    )
```

profile of v0, /device:TPU:5, one launch (start us, length us, event | category | flops | bytes accessed | tf_op | source)
XLA Modules:
  0.0 191.8 jit_solution(1654663557395081504)
XLA Ops:
  6.5 0.7 all-gather.3.cloned.1.call-update
  7.3 0.7 all-gather.5.cloned.1.call-update
  8.1 1.1 copy.16
  9.3 0.8 reduce-window.8
  10.3 0.7 select_reduce_fusion
  11.0 54.3 %all-gather.3.cloned.1.call-done = bf16[1,4096,128]{2,1,0:T(8,128)(2,1)} async-done(((bf16[1,256,128]{2,1,0:T(8,128)(2,1)}), bf16[1,4096,128]{2,1,0:T(8,128)(2,1)}) %all-gather.3.cloned.1.call-update) | async-done | bytes 1048592 | tf_op jit(solution)/shard_map/all_gather | solution.py:61
  65.3 56.9 %all-gather.5.cloned.1.call-done = bf16[1,4096,128]{2,1,0:T(8,128)(2,1)} async-done(((bf16[1,256,128]{2,1,0:T(8,128)(2,1)}), bf16[1,4096,128]{2,1,0:T(8,128)(2,1)}) %all-gather.5.cloned.1.call-update) | async-done | bytes 1048592 | tf_op jit(solution)/shard_map/all_gather | solution.py:62
  122.3 39.0 %while.21 = (s32[]{:T(128)}, f32[2,8,128]{2,1,0:T(8,128)S(1)}, f32[2,8,128]{2,1,0:T(8,128)S(1)}, f32[2,128,8,128]{3,1,2,0:T(8,128)S(1)}, s32[2,128]{1,0:T(2,128)...) while((s32[]{:T(128)}, f32[2,8,128]{2,1,0:T(8,128)S(1)}, ...), condition=%wide.region_8.9_spmd.clone, body=%wide.region_2.8_spmd.clone.sunk | while | flops 1102629120 | bytes 29502764 | solution.py:92
  122.4 1.0 compare_and_fusion.2
  124.0 8.0 %conditional.3 = ((f32[2,8,128]{2,1,0:T(8,128)S(1)}, f32[2,8,128]{2,1,0:T(8,128)S(1)}, f32[2,128,8,128]{3,1,2,0:T(8,128)S(1)})) conditional(s32[]{:T(128)} %convert_element_type.36, (f32[2,8,128]{2,1,0:T(8,128)S(1)}, f32[2,8,128]{2,1,0:T(8,128)S(1)}, f32[2,128,8,128]{3,1,2,0:T(8,128)S(1)}) %tuple.70, (pred[2,128,1024]{1,2,0:T(8,128)(4,1)S(1)}, ...), branch_computations={%region_4.4_spmd, %region_5.7_spmd} | conditional | flops 1101535232 | bytes 29229130 | solution.py:54
  124.0 2.3 %fusion.4 = (f32[2,8,128]{2,1,0:T(8,128)S(1)}, f32[1024,2,128,8]{2,0,3,1:T(8,128)S(1)}) fusion(pred[2,128,1024]{1,2,0:T(8,128)(4,1)S(1)} %get-tuple-element.392, bf16[2,128,8,128]{3,1,2,0:T(8,128)(2,1)S(1)} %get-tuple-element.395, bf16[1,4096,128]{2,1,0:T(8,128)(2,1)} %get-tuple-element.393, s32[]{:T(128)S(6)} %select_n.112), kind=kOutput, calls=%fused_computation.4 | convolution fusion | flops 543160320 | bytes 9445380 | tf_op jit(solution)/shard_map/while/body/eval_jaxpr/cond/branch_1_fun/sihd,jd->shij/dot_general | solution.py:35
  126.3 3.6 %fusion.13 = f32[2,128,8,128]{3,1,2,0:T(8,128)S(1)} fusion(f32[1024,2,128,8]{2,0,3,1:T(8,128)S(1)} %get-tuple-element.481, f32[2,8,128]{2,1,0:T(8,128)S(1)} %get-tuple-element.552, pred[2,128,1024]{1,2,0:T(8,128)(4,1)S(1)} %get-tuple-element.392, f32[2,128,8,128]{3,1,2,0:T(8,128)S(1)} %get-tuple-element.397, f32[2,128,8]{1,2,0:T(8,128)S(1)} %get-tuple-element.478, ...), kind=kOutput, calls=%fused_computation.10 | convolution fusion | flops 547880960 | bytes 11026436 | tf_op jit(solution)/shard_map/while/body/eval_jaxpr/cond/branch_1_fun/shij,jd->sihd/dot_general | solution.py:45
  130.0 2.0 %fusion.6 = f32[2,8,128]{2,1,0:T(8,128)S(1)} fusion(f32[1024,2,128,8]{2,0,3,1:T(8,128)S(1)} %get-tuple-element.481, f32[2,8,128]{2,1,0:T(8,128)S(1)} %get-tuple-element.552, pred[2,128,1024]{1,2,0:T(8,128)(4,1)S(1)} %get-tuple-element.392), kind=kLoop, calls=%fused_computation.6 | loop fusion | flops 10483712 | bytes 8667136 | tf_op jit(solution)/shard_map/while/body/eval_jaxpr/cond/branch_1_fun/reduce_sum | solution.py:44
  132.2 1.0 compare_and_fusion.2
  133.8 8.0 %conditional.3 = ((f32[2,8,128]{2,1,0:T(8,128)S(1)}, f32[2,8,128]{2,1,0:T(8,128)S(1)}, f32[2,128,8,128]{3,1,2,0:T(8,128)S(1)})) conditional(s32[]{:T(128)} %convert_element_type.36, (f32[2,8,128]{2,1,0:T(8,128)S(1)}, f32[2,8,128]{2,1,0:T(8,128)S(1)}, f32[2,128,8,128]{3,1,2,0:T(8,128)S(1)}) %tuple.70, (pred[2,128,1024]{1,2,0:T(8,128)(4,1)S(1)}, ...), branch_computations={%region_4.4_spmd, %region_5.7_spmd} | conditional | flops 1101535232 | bytes 29229130 | solution.py:54
  133.8 2.3 %fusion.4 = (f32[2,8,128]{2,1,0:T(8,128)S(1)}, f32[1024,2,128,8]{2,0,3,1:T(8,128)S(1)}) fusion(pred[2,128,1024]{1,2,0:T(8,128)(4,1)S(1)} %get-tuple-element.392, bf16[2,128,8,128]{3,1,2,0:T(8,128)(2,1)S(1)} %get-tuple-element.395, bf16[1,4096,128]{2,1,0:T(8,128)(2,1)} %get-tuple-element.393, s32[]{:T(128)S(6)} %select_n.112), kind=kOutput, calls=%fused_computation.4 | convolution fusion | flops 543160320 | bytes 9445380 | tf_op jit(solution)/shard_map/while/body/eval_jaxpr/cond/branch_1_fun/sihd,jd->shij/dot_general | solution.py:35
  136.1 3.6 %fusion.13 = f32[2,128,8,128]{3,1,2,0:T(8,128)S(1)} fusion(f32[1024,2,128,8]{2,0,3,1:T(8,128)S(1)} %get-tuple-element.481, f32[2,8,128]{2,1,0:T(8,128)S(1)} %get-tuple-element.552, pred[2,128,1024]{1,2,0:T(8,128)(4,1)S(1)} %get-tuple-element.392, f32[2,128,8,128]{3,1,2,0:T(8,128)S(1)} %get-tuple-element.397, f32[2,128,8]{1,2,0:T(8,128)S(1)} %get-tuple-element.478, ...), kind=kOutput, calls=%fused_computation.10 | convolution fusion | flops 547880960 | bytes 11026436 | tf_op jit(solution)/shard_map/while/body/eval_jaxpr/cond/branch_1_fun/shij,jd->sihd/dot_general | solution.py:45
  139.7 2.0 %fusion.6 = f32[2,8,128]{2,1,0:T(8,128)S(1)} fusion(f32[1024,2,128,8]{2,0,3,1:T(8,128)S(1)} %get-tuple-element.481, f32[2,8,128]{2,1,0:T(8,128)S(1)} %get-tuple-element.552, pred[2,128,1024]{1,2,0:T(8,128)(4,1)S(1)} %get-tuple-element.392), kind=kLoop, calls=%fused_computation.6 | loop fusion | flops 10483712 | bytes 8667136 | tf_op jit(solution)/shard_map/while/body/eval_jaxpr/cond/branch_1_fun/reduce_sum | solution.py:44
  141.9 1.0 compare_and_fusion.2
  143.5 8.0 %conditional.3 = ((f32[2,8,128]{2,1,0:T(8,128)S(1)}, f32[2,8,128]{2,1,0:T(8,128)S(1)}, f32[2,128,8,128]{3,1,2,0:T(8,128)S(1)})) conditional(s32[]{:T(128)} %convert_element_type.36, (f32[2,8,128]{2,1,0:T(8,128)S(1)}, f32[2,8,128]{2,1,0:T(8,128)S(1)}, f32[2,128,8,128]{3,1,2,0:T(8,128)S(1)}) %tuple.70, (pred[2,128,1024]{1,2,0:T(8,128)(4,1)S(1)}, ...), branch_computations={%region_4.4_spmd, %region_5.7_spmd} | conditional | flops 1101535232 | bytes 29229130 | solution.py:54
  143.5 2.3 %fusion.4 = (f32[2,8,128]{2,1,0:T(8,128)S(1)}, f32[1024,2,128,8]{2,0,3,1:T(8,128)S(1)}) fusion(pred[2,128,1024]{1,2,0:T(8,128)(4,1)S(1)} %get-tuple-element.392, bf16[2,128,8,128]{3,1,2,0:T(8,128)(2,1)S(1)} %get-tuple-element.395, bf16[1,4096,128]{2,1,0:T(8,128)(2,1)} %get-tuple-element.393, s32[]{:T(128)S(6)} %select_n.112), kind=kOutput, calls=%fused_computation.4 | convolution fusion | flops 543160320 | bytes 9445380 | tf_op jit(solution)/shard_map/while/body/eval_jaxpr/cond/branch_1_fun/sihd,jd->shij/dot_general | solution.py:35
  145.8 3.6 %fusion.13 = f32[2,128,8,128]{3,1,2,0:T(8,128)S(1)} fusion(f32[1024,2,128,8]{2,0,3,1:T(8,128)S(1)} %get-tuple-element.481, f32[2,8,128]{2,1,0:T(8,128)S(1)} %get-tuple-element.552, pred[2,128,1024]{1,2,0:T(8,128)(4,1)S(1)} %get-tuple-element.392, f32[2,128,8,128]{3,1,2,0:T(8,128)S(1)} %get-tuple-element.397, f32[2,128,8]{1,2,0:T(8,128)S(1)} %get-tuple-element.478, ...), kind=kOutput, calls=%fused_computation.10 | convolution fusion | flops 547880960 | bytes 11026436 | tf_op jit(solution)/shard_map/while/body/eval_jaxpr/cond/branch_1_fun/shij,jd->sihd/dot_general | solution.py:45
  149.5 2.0 %fusion.6 = f32[2,8,128]{2,1,0:T(8,128)S(1)} fusion(f32[1024,2,128,8]{2,0,3,1:T(8,128)S(1)} %get-tuple-element.481, f32[2,8,128]{2,1,0:T(8,128)S(1)} %get-tuple-element.552, pred[2,128,1024]{1,2,0:T(8,128)(4,1)S(1)} %get-tuple-element.392), kind=kLoop, calls=%fused_computation.6 | loop fusion | flops 10483712 | bytes 8667136 | tf_op jit(solution)/shard_map/while/body/eval_jaxpr/cond/branch_1_fun/reduce_sum | solution.py:44
  151.6 1.0 compare_and_fusion.2
  153.2 8.0 %conditional.3 = ((f32[2,8,128]{2,1,0:T(8,128)S(1)}, f32[2,8,128]{2,1,0:T(8,128)S(1)}, f32[2,128,8,128]{3,1,2,0:T(8,128)S(1)})) conditional(s32[]{:T(128)} %convert_element_type.36, (f32[2,8,128]{2,1,0:T(8,128)S(1)}, f32[2,8,128]{2,1,0:T(8,128)S(1)}, f32[2,128,8,128]{3,1,2,0:T(8,128)S(1)}) %tuple.70, (pred[2,128,1024]{1,2,0:T(8,128)(4,1)S(1)}, ...), branch_computations={%region_4.4_spmd, %region_5.7_spmd} | conditional | flops 1101535232 | bytes 29229130 | solution.py:54
  153.3 2.3 %fusion.4 = (f32[2,8,128]{2,1,0:T(8,128)S(1)}, f32[1024,2,128,8]{2,0,3,1:T(8,128)S(1)}) fusion(pred[2,128,1024]{1,2,0:T(8,128)(4,1)S(1)} %get-tuple-element.392, bf16[2,128,8,128]{3,1,2,0:T(8,128)(2,1)S(1)} %get-tuple-element.395, bf16[1,4096,128]{2,1,0:T(8,128)(2,1)} %get-tuple-element.393, s32[]{:T(128)S(6)} %select_n.112), kind=kOutput, calls=%fused_computation.4 | convolution fusion | flops 543160320 | bytes 9445380 | tf_op jit(solution)/shard_map/while/body/eval_jaxpr/cond/branch_1_fun/sihd,jd->shij/dot_general | solution.py:35
  155.6 3.6 %fusion.13 = f32[2,128,8,128]{3,1,2,0:T(8,128)S(1)} fusion(f32[1024,2,128,8]{2,0,3,1:T(8,128)S(1)} %get-tuple-element.481, f32[2,8,128]{2,1,0:T(8,128)S(1)} %get-tuple-element.552, pred[2,128,1024]{1,2,0:T(8,128)(4,1)S(1)} %get-tuple-element.392, f32[2,128,8,128]{3,1,2,0:T(8,128)S(1)} %get-tuple-element.397, f32[2,128,8]{1,2,0:T(8,128)S(1)} %get-tuple-element.478, ...), kind=kOutput, calls=%fused_computation.10 | convolution fusion | flops 547880960 | bytes 11026436 | tf_op jit(solution)/shard_map/while/body/eval_jaxpr/cond/branch_1_fun/shij,jd->sihd/dot_general | solution.py:45
  159.2 2.0 %fusion.6 = f32[2,8,128]{2,1,0:T(8,128)S(1)} fusion(f32[1024,2,128,8]{2,0,3,1:T(8,128)S(1)} %get-tuple-element.481, f32[2,8,128]{2,1,0:T(8,128)S(1)} %get-tuple-element.552, pred[2,128,1024]{1,2,0:T(8,128)(4,1)S(1)} %get-tuple-element.392), kind=kLoop, calls=%fused_computation.6 | loop fusion | flops 10483712 | bytes 8667136 | tf_op jit(solution)/shard_map/while/body/eval_jaxpr/cond/branch_1_fun/reduce_sum | solution.py:44
  161.3 0.3 divide_convert_fusion
  161.6 0.3 copy.12
  162.0 11.8 %convolution_convert_fusion = bf16[256,8192]{1,0:T(8,128)(2,1)} fusion(bf16[1024,8192]{1,0:T(8,128)(2,1)} %param.13, bf16[32,8,8,128]{3,2,1,0:T(8,128)(2,1)S(1)} %bitcast.55), kind=kOutput, calls=%fused_computation.54 | convolution fusion | flops 4297064448 | bytes 21495808 | tf_op jit(solution)/shard_map/dot_general | solution.py:97
  173.8 11.5 %reduce-scatter.2.cloned.1.call-done = bf16[128,8192]{1,0:T(8,128)(2,1)} async-done(((bf16[256,8192]{1,0:T(8,128)(2,1)}), bf16[128,8192]{1,0:T(8,128)(2,1)}) %reduce-scatter.2.cloned.1.call-update) | async-done | bytes 2097168 | tf_op jit(solution)/shard_map/reduce_scatter | solution.py:96
  (30 shorter events, 0.9 us)
Async XLA Ops:
  6.5 58.8 %all-gather.3.cloned.1.call-start = ((), (), s32[]{:S(2)}) async-start(), calls=%async_computation.1 | async-start | bytes 1114112 | tf_op jit(solution)/shard_map/all_gather | solution.py:61
  7.3 114.9 %all-gather.5.cloned.1.call-start = ((), (), s32[]{:S(2)}) async-start(), calls=%async_computation.2 | async-start | bytes 1114112 | tf_op jit(solution)/shard_map/all_gather | solution.py:62
  8.0 177.3 %reduce-scatter.2.cloned.1.call-start = ((), (), s32[]{:S(2)}) async-start(), calls=%async_computation.3 | async-start | bytes 6291456 | tf_op jit(solution)/shard_map/reduce_scatter | solution.py:96
Sparse Core Ops, SparseCore 0:
  10.1 55.1 all-gather.2
  68.1 54.0 all-gather.4
  173.9 11.3 reduce-scatter.1
where the time goes:
time: 190 us; the launch traced here: 192 us
  waiting for transfers between devices  124 us (65%)
  matrix products  35.4 us (19%)
  other arithmetic  14.5 us (8%)
  between operations  13.2 us (7%)
  loops' own time  2.86 us (2%)
    all_gather x1, waiting for transfers between devices, on_device(): value_piece = lax.all_gather(values, 'ctx', axis=1, tiled=True)  56.9 us
    all_gather x1, waiting for transfers between devices, on_device(): key_piece = lax.all_gather(keys, 'ctx', axis=1, tiled=True)  54.3 us
    dot_general x4, matrix products, absorb(): jnp.einsum('shij,jd->sihd', weights.astype(jnp.bfloat16), value_tile[0],...  14.5 us
    dot_general x1, matrix products, on_device(): jnp.dot(attended, w_out, preferred_element_type=jnp.float32)  11.8 us
    reduce_scatter x1, waiting for transfers between devices, on_device(): lax.psum_scatter(jnp.dot(attended, w_out, preferred_element_type=jnp.floa...  11.5 us
    dot_general x4, matrix products, absorb(): jnp.einsum('sihd,jd->shij', slot_queries, key_tile[0], preferred_element_...  9.12 us
    reduce_sum x4, other arithmetic, absorb(): denominator = denominator * rescale + jnp.sum(weights, axis=3)  8.09 us
    and x4, other arithmetic, update(): (key_pos[:, None, :] <= slot_pos[:, :, None]) & (key_pos[:, None, :] >= s...  3.92 us
  transfers between devices with their start and end apart: 3, of which 3 were waited for; matrix products, arithmetic and copies ran while one was open for 2% of the time, Pallas kernels for 0%

commit v1 on v0

v1 whole, which is shorter than its diff:
```python
import functools
import math

import jax
import jax.numpy as jnp
from jax import lax
from jax.experimental import pallas as pl
from jax.experimental.pallas import tpu as pltpu
from jax.sharding import PartitionSpec as P

MESH = pl.DeviceIdType.MESH
NEG = -1e30
FLOOR = -1e20
COLUMNS = 512
LAG = 2


def grid_of(n):
    z = 4 if n % 4 == 0 else 1
    rest = n // z
    x = max(i for i in range(1, math.isqrt(rest) + 1) if rest % i == 0)
    return z, rest // x, x


def nearest(p, k, size):
    m = jnp.minimum(p, size - 1 - p)
    half = (k + 1) // 2
    near = jnp.where(k % 2 == 1, p + half, p - half)
    far = jnp.where(p < size - 1 - p, k, size - 1 - k)
    return jnp.where(k <= 2 * m, near, far)


def kernel(
    n,
    docs,
    lengths,
    q_hbm,
    k_ref,
    v_ref,
    w_hbm,
    out_hbm,
    kv,
    q_in,
    q_t,
    top,
    den,
    acc,
    att,
    w,
    mine,
    outgoing,
    incoming,
    result,
    local_sem,
    send_sem,
    recv_sem,
    part_send,
    part_recv,
    out_sem,
):
    sizes = grid_of(n)
    Z, Y, X = sizes
    block = k_ref.shape[1] // 2
    hd = k_ref.shape[2]
    width = q_in.shape[1]
    heads = width // hd
    me = lax.axis_index("ctx")
    core = lax.axis_index("kvh")
    place = (me // (Y * X), (me // X) % Y, me % X)
    strides = (Y * X, X, 1)

    q_copy = pltpu.make_async_copy(q_hbm.at[0], q_in, local_sem.at[0])
    q_copy.start()
    w_copy = pltpu.make_async_copy(w_hbm, w, local_sem.at[1])

    barrier = pltpu.get_barrier_semaphore()
    count = jnp.int32(1)
    pl.semaphore_signal(
        barrier, inc=1, device_id={"kvh": 1 - core}, device_id_type=MESH
    )
    for axis in range(3):
        for step in (1, -1):
            there = place[axis] + step
            exists = (there >= 0) & (there < sizes[axis])
            count = count + exists.astype(jnp.int32)

            @pl.when(exists)
            def _(axis=axis, step=step):
                pl.semaphore_signal(
                    barrier,
                    inc=1,
                    device_id={"ctx": me + step * strides[axis]},
                    device_id_type=MESH,
                )

    for b in range(2):
        kv[me, b, 0:block] = k_ref[0, b * block : (b + 1) * block]
        kv[me, b, block:] = v_ref[0, b * block : (b + 1) * block].T
    pl.semaphore_wait(barrier, count)

    def wanted(b, source, low, high):
        if b == 0:
            return high >= jnp.minimum(source, n - 1 - source)
        return low <= source

    def index(coords):
        return sum(c * s for c, s in zip(coords, strides))

    def tree(source, b):
        order = (0, 2, 1) if b == 0 else (0, 1, 2)
        src = (source // (Y * X), (source // X) % Y, source % X)
        edges = []
        arrives = jnp.bool_(False)
        on_line = jnp.bool_(True)
        for depth in (2, 1, 0):
            axis = order[depth]
            inner = order[depth + 1 :]
            p, s = place[axis], src[axis]
            first, last = list(place), list(place)
            for a in inner:
                first[a], last[a] = 0, sizes[a] - 1
            for step in (1, -1):
                there = p + step
                first_a, last_a = (there, sizes[axis] - 1) if step == 1 else (0, there)
                first[axis], last[axis] = first_a, last_a
                exists = (there >= 0) & (there < sizes[axis])
                onward = (p >= s) if step == 1 else (p <= s)
                go = on_line & exists & onward
                go = go & wanted(b, source, index(first), index(last))
                edges.append((go, axis * 2 + (step == 1), me + step * strides[axis]))
                first[axis], last[axis] = (p, sizes[axis] - 1) if step == 1 else (0, p)
                passed = (p > s) if step == 1 else (p < s)
                arrives = arrives | (
                    on_line & passed & wanted(b, source, index(first), index(last))
                )
            on_line = on_line & (p == s)
        return edges, arrives

    def copy_of(source, b, way, target):
        return pltpu.make_async_remote_copy(
            src_ref=kv.at[source, b],
            dst_ref=kv.at[source, b],
            send_sem=send_sem.at[source, b, way],
            recv_sem=recv_sem.at[source, b],
            device_id={"ctx": target},
            device_id_type=MESH,
        )

    def pass_on(source):
        for b in range(2):
            edges, arrives = tree(source, b)

            @pl.when(arrives)
            def _(b=b):
                copy_of(source, b, 0, me).wait_recv()

            for go, way, target in reversed(edges):

                @pl.when(go)
                def _(b=b, way=way, target=target):
                    copy_of(source, b, way, target).start()

    pass_on(me)
    w_copy.start()

    q_copy.wait()
    for b in range(2):
        for h in range(heads):
            q_t[b, :, h * hd : (h + 1) * hd] = q_in[
                b * block : (b + 1) * block, h * hd : (h + 1) * hd
            ].T
    top[...] = jnp.full(top.shape, FLOOR, jnp.float32)
    den[...] = jnp.zeros(den.shape, jnp.float32)
    acc[...] = jnp.zeros(acc.shape, jnp.float32)

    own_blocks = (me, 2 * n - 1 - me)
    lanes = lax.broadcasted_iota(jnp.int32, (1, block), 1)
    query_pos = [c * block + lanes for c in own_blocks]
    doc_start = [jnp.zeros((1, block), jnp.int32) for _ in own_blocks]
    end = jnp.int32(0)
    for i in range(docs):
        length = lengths[i]
        end = end + length
        doc_start = [
            s + jnp.where(end <= p, length, 0) for s, p in zip(doc_start, query_pos)
        ]

    factor = hd ** (-0.5) * math.log2(math.e)
    rows = lax.broadcasted_iota(jnp.int32, (block, block), 0)
    group = 2 * hd if heads % 2 == 0 else hd

    def absorb(qb, source, blocks):
        biases, keys, vals = [], [], []
        for b in blocks:
            c = source if b == 0 else 2 * n - 1 - source
            key_pos = c * block + rows
            allowed = (key_pos <= query_pos[qb]) & (key_pos >= doc_start[qb])
            biases.append(jnp.where(allowed, 0.0, NEG))
            keys.append(kv[source, b, 0:block])
            vals.append(kv[source, b, block:])
        bias = jnp.concatenate(biases, axis=0) if len(blocks) > 1 else biases[0]
        bias = jnp.concatenate([bias] * (group // block), axis=1)
        key = jnp.concatenate(keys, axis=0) if len(blocks) > 1 else keys[0]
        val = jnp.concatenate(vals, axis=1) if len(blocks) > 1 else vals[0]
        for c in range(width // group):
            cols = slice(c * group, (c + 1) * group)
            scores = jnp.dot(key, q_t[qb, :, cols], preferred_element_type=jnp.float32)
            scores = scores + bias
            old = top[qb, :, cols]
            new = jnp.maximum(old, jnp.max(scores, axis=0, keepdims=True))
            weights = jnp.exp2((scores - new) * factor)
            rescale = jnp.exp2((old - new) * factor)
            top[qb, :, cols] = new
            den[qb, :, cols] = den[qb, :, cols] * rescale + jnp.sum(
                weights, axis=0, keepdims=True
            )
            acc[qb, :, cols] = acc[qb, :, cols] * rescale + jnp.dot(
                val, weights.astype(jnp.bfloat16), preferred_element_type=jnp.float32
            )

    plane = Y * X

    def source_at(kz, j):
        return index(
            (
                nearest(place[0], kz, Z),
                nearest(place[1], j // X, Y),
                nearest(place[2], j % X, X),
            )
        )

    def visit(r, carry):
        kz, j = r // plane, r % plane
        source = source_at(kz, j)

        @pl.when((j == 0) & (kz + 1 < Z))
        def _():
            pass_on(source_at(kz + 1, 0))

        @pl.when(j > 0)
        def _():
            pass_on(source)

        low = source >= n - 1 - me
        high = source >= me

        @pl.when(source <= me)
        def _():
            absorb(0, source, (0,))

        @pl.when(low & high)
        def _():
            absorb(1, source, (0, 1))

        @pl.when(low & jnp.logical_not(high))
        def _():
            absorb(1, source, (0,))

        @pl.when(high & jnp.logical_not(low))
        def _():
            absorb(1, source, (1,))

        return carry

    lax.fori_loop(0, n, visit, 0)

    for qb in range(2):
        spot = (1 - core) if qb == 0 else core
        at = pl.multiple_of(spot * block, block)
        for h in range(heads):
            cols = slice(h * hd, (h + 1) * hd)
            o = acc[qb, :, cols] / den[qb, :, cols]
            att[pl.ds(at, block), cols] = o.T.astype(jnp.bfloat16)

    w_copy.wait()
    chunks = w.shape[1] // COLUMNS

    def part(j):
        return pltpu.make_async_remote_copy(
            src_ref=outgoing.at[j],
            dst_ref=incoming.at[j],
            send_sem=part_send.at[j],
            recv_sem=part_recv.at[j],
            device_id={"kvh": 1 - core},
            device_id_type=MESH,
        )

    def store(j):
        at = pl.multiple_of(j * COLUMNS, COLUMNS)
        return pltpu.make_async_copy(
            result.at[j], out_hbm.at[:, pl.ds(at, COLUMNS)], out_sem.at[j]
        )

    def finish(j):
        part(j).wait_recv()
        total = mine[j] + incoming[j].astype(jnp.float32)
        result[j] = total.astype(jnp.bfloat16)
        store(j).start()

    def project(j, carry):
        at = pl.multiple_of(j * COLUMNS, COLUMNS)
        both = jnp.dot(
            att[...], w[:, pl.ds(at, COLUMNS)], preferred_element_type=jnp.float32
        )
        outgoing[j] = both[:block].astype(jnp.bfloat16)
        part(j).start()
        mine[j] = both[block:]

        @pl.when(j >= LAG)
        def _():
            finish(j - LAG)

        return carry

    lax.fori_loop(0, chunks, project, 0)

    def tail(j, carry):
        finish(j)
        return carry

    lax.fori_loop(chunks - LAG, chunks, tail, 0)

    def sent(source, carry):
        for b in range(2):
            for go, way, target in tree(source, b)[0]:

                @pl.when(go)
                def _(b=b, way=way, target=target):
                    copy_of(source, b, way, target).wait_send()

        return carry

    lax.fori_loop(0, n, sent, 0)

    def stored(j, carry):
        part(j).wait_send()
        store(j).wait()
        return carry

    lax.fori_loop(0, chunks, stored, 0)


def on_device(n, queries, keys, values, doc_lengths, w_out):
    rows, hd = keys.shape[1:]
    width = queries.shape[2]
    block = rows // 2
    model = w_out.shape[1]
    chunks = model // COLUMNS
    vmem = pl.BlockSpec(memory_space=pltpu.VMEM)
    far = pl.BlockSpec(memory_space=pl.ANY)
    pairs = 2 * n + 2
    return pl.pallas_call(
        functools.partial(kernel, n, doc_lengths.shape[0]),
        out_shape=jax.ShapeDtypeStruct((block, model), jnp.bfloat16),
        in_specs=[pl.BlockSpec(memory_space=pltpu.SMEM), far, vmem, vmem, far],
        out_specs=far,
        scratch_shapes=[
            pltpu.VMEM((n, 2, 2 * block, hd), jnp.bfloat16),
            pltpu.VMEM((rows, width), jnp.bfloat16),
            pltpu.VMEM((2, hd, width), jnp.bfloat16),
            pltpu.VMEM((2, 1, width), jnp.float32),
            pltpu.VMEM((2, 1, width), jnp.float32),
            pltpu.VMEM((2, hd, width), jnp.float32),
            pltpu.VMEM((rows, width), jnp.bfloat16),
            pltpu.VMEM(w_out.shape, jnp.bfloat16),
            pltpu.VMEM((chunks, block, COLUMNS), jnp.float32),
            pltpu.VMEM((chunks, block, COLUMNS), jnp.bfloat16),
            pltpu.VMEM((chunks, block, COLUMNS), jnp.bfloat16),
            pltpu.VMEM((chunks, block, COLUMNS), jnp.bfloat16),
            pltpu.SemaphoreType.DMA((2,)),
            pltpu.SemaphoreType.DMA((n, 2, 6)),
            pltpu.SemaphoreType.DMA((n, 2)),
            pltpu.SemaphoreType.DMA((chunks,)),
            pltpu.SemaphoreType.DMA((chunks,)),
            pltpu.SemaphoreType.DMA((chunks,)),
        ],
        compiler_params=pltpu.CompilerParams(
            collective_id=0, has_side_effects=True, vmem_limit_bytes=56 * 1024 * 1024
        ),
        cost_estimate=pl.CostEstimate(
            flops=4 * pairs * block * block * width + 2 * rows * width * model,
            bytes_accessed=2 * (w_out.size + block * model),
            transcendentals=pairs * block * width,
        ),
        name="attend_and_project",
    )(doc_lengths, queries, keys, values, w_out)


def solution(mesh):
    in_specs = (
        P("kvh", "ctx", None),
        P("kvh", "ctx", None),
        P("kvh", "ctx", None),
        P(),
        P("kvh", None),
    )
    out_specs = P(("ctx", "kvh"), None)
    return jax.shard_map(
        functools.partial(on_device, mesh.shape["ctx"]),
        mesh=mesh,
        in_specs=in_specs,
        out_specs=out_specs,
        check_vma=False,
    )
```

time: 190 us -> 53.5 us (0.28); the launches traced: 192 us -> 53.3 us
  waiting for transfers between devices: 124 us -> 0 us
  Pallas kernels: 0 us -> 50.2 us
  matrix products: 35.4 us -> 0 us
  other arithmetic: 14.5 us -> 0 us
  between operations: 13.2 us -> 0.01 us
  loops' own time: 2.86 us -> 0 us
    all_gather x2 -> x0, waiting for transfers between devices: 111 us -> none  [the longest x1 56.9 us: on_device(): value_piece = lax.all_gather(values, 'ctx', axis=1, tiled=True)]
    pallas_call x0 -> x1, Pallas kernels: none -> 50.2 us  [on_device(): pl.pallas_call(functools.partial(kernel, n, doc_lengths.shape[0]), out_sh...]
    dot_general x9 -> x0, matrix products: 35.4 us -> none  [the longest x4 14.5 us: absorb(): jnp.einsum('shij,jd->sihd', weights.astype(jnp.bfloat16), value_tile[0],...]
    reduce_scatter x1 -> x0, waiting for transfers between devices: 11.5 us -> none  [on_device(): lax.psum_scatter(jnp.dot(attended, w_out, preferred_element_type=jnp.floa...]
    reduce_sum x5 -> x0, other arithmetic: 8.83 us -> none  [the longest x4 8.09 us: absorb(): denominator = denominator * rescale + jnp.sum(weights, axis=3)]
    and x4 -> x0, other arithmetic: 3.92 us -> none  [update(): (key_pos[:, None, :] <= slot_pos[:, :, None]) & (key_pos[:, None, :] >= s...]
    another operation x5 -> x0, loops' own time: 2.86 us -> none  [the longest x1 2.6 us: on_device(): state = lax.fori_loop(0, shard_count // per_step, absorb_tile, initial)]
  transfers between devices with their start and end apart: 3 -> 0, of which waited for: 3 -> 0; matrix products, arithmetic and copies ran while one was open for 2% -> 0% of each run, Pallas kernels for 0% -> 0%
where the time goes in v1:
time: 53.5 us; the launch traced here: 53.3 us
  Pallas kernels  50.2 us (94%)
  local copies, waits for them, and re-layouts  3.1 us (6%)
    pallas_call x1, Pallas kernels, on_device(): pl.pallas_call(functools.partial(kernel, n, doc_lengths.shape[0]), out_sh...  50.2 us
    unnamed x1, local copies, waits for them, and re-layouts  3.1 us

profile of v1, /device:TPU:5, one launch (start us, length us, event | category | flops | bytes accessed | tf_op | source)
XLA Modules:
  0.0 53.3 jit_solution(6107679410790049045)
XLA Ops:
  0.0 50.2 %attend_and_project.1 = bf16[128,8192]{1,0:T(8,128)(2,1)} custom-call(s32[8]{0:T(128)} %lengths.1, bf16[1,256,1024]{2,1,0:T(8,128)(2,1)} %q_hbm.1, bf16[1,256,128]{2,1,0:T(8,128)(2,1)} %k_ref.1, bf16[1,256,128]{2,1,0:T(8,128)(2,1)} %v_ref.1, bf16[1024,8192]{1,0:T(8,128)(2,1)} %w_hbm.1), custom_call_target="tpu_custom_call" | custom-call | flops 6576668672 | bytes 18874368 | tf_op jit(solution)/shard_map/attend_and_project/pallas_call | solution.py:352
  50.3 3.1 %copy.7 = bf16[128,8192]{1,0:T(8,128)(2,1)} copy(bf16[128,8192]{1,0:T(8,128)(2,1)} %attend_and_project.1) | data formatting | bytes 4194304

commit v2 on v1

--- a/solution.py
+++ b/solution.py
@@ -99,9 +99,10 @@
     pl.semaphore_wait(barrier, count)
 
     def wanted(b, source, low, high):
+        pair = source // 2
         if b == 0:
-            return high >= jnp.minimum(source, n - 1 - source)
-        return low <= source
+            return high >= jnp.minimum(2 * pair, n - 2 - 2 * pair)
+        return low <= 2 * pair + 1
 
     def index(coords):
         return sum(c * s for c, s in zip(coords, strides))
@@ -189,19 +190,19 @@
     rows = lax.broadcasted_iota(jnp.int32, (block, block), 0)
     group = 2 * hd if heads % 2 == 0 else hd
 
-    def absorb(qb, source, blocks):
+    def absorb(qb, pair, b):
         biases, keys, vals = [], [], []
-        for b in blocks:
+        for source in (2 * pair, 2 * pair + 1):
             c = source if b == 0 else 2 * n - 1 - source
             key_pos = c * block + rows
             allowed = (key_pos <= query_pos[qb]) & (key_pos >= doc_start[qb])
             biases.append(jnp.where(allowed, 0.0, NEG))
             keys.append(kv[source, b, 0:block])
             vals.append(kv[source, b, block:])
-        bias = jnp.concatenate(biases, axis=0) if len(blocks) > 1 else biases[0]
+        bias = jnp.concatenate(biases, axis=0)
         bias = jnp.concatenate([bias] * (group // block), axis=1)
-        key = jnp.concatenate(keys, axis=0) if len(blocks) > 1 else keys[0]
-        val = jnp.concatenate(vals, axis=1) if len(blocks) > 1 else vals[0]
+        key = jnp.concatenate(keys, axis=0)
+        val = jnp.concatenate(vals, axis=1)
         for c in range(width // group):
             cols = slice(c * group, (c + 1) * group)
             scores = jnp.dot(key, q_t[qb, :, cols], preferred_element_type=jnp.float32)
@@ -221,16 +222,17 @@
     plane = Y * X
 
     def source_at(kz, j):
+        x, kx = place[2], j % X
         return index(
             (
                 nearest(place[0], kz, Z),
                 nearest(place[1], j // X, Y),
-                nearest(place[2], j % X, X),
+                nearest(x // 2, kx // 2, X // 2) * 2 + (x + kx) % 2,
             )
         )
 
     def visit(r, carry):
-        kz, j = r // plane, r % plane
+        kz, j = r // (plane // 2), 2 * (r % (plane // 2))
         source = source_at(kz, j)
 
         @pl.when((j == 0) & (kz + 1 < Z))
@@ -241,28 +243,24 @@
         def _():
             pass_on(source)
 
-        low = source >= n - 1 - me
-        high = source >= me
-
-        @pl.when(source <= me)
-        def _():
-            absorb(0, source, (0,))
-
-        @pl.when(low & high)
-        def _():
-            absorb(1, source, (0, 1))
-
-        @pl.when(low & jnp.logical_not(high))
-        def _():
-            absorb(1, source, (0,))
-
-        @pl.when(high & jnp.logical_not(low))
-        def _():
-            absorb(1, source, (1,))
+        pass_on(source_at(kz, j + 1))
+        pair = source // 2
+
+        @pl.when(2 * pair <= me)
+        def _():
+            absorb(0, pair, 0)
+
+        @pl.when(2 * pair + 1 >= n - 1 - me)
+        def _():
+            absorb(1, pair, 0)
+
+        @pl.when(2 * pair + 1 >= me)
+        def _():
+            absorb(1, pair, 1)
 
         return carry
 
-    lax.fori_loop(0, n, visit, 0)
+    lax.fori_loop(0, n // 2, visit, 0)
 
     for qb in range(2):
         spot = (1 - core) if qb == 0 else core

time: 53.5 us -> 57.6 us (1.077)
  Pallas kernels: 50.2 us -> 54 us
    pallas_call x1, Pallas kernels: 50.2 us -> 54 us  [on_device(): pl.pallas_call(functools.partial(kernel, n, doc_lengths.shape[0]), out_sh...]
where the time goes in v2:
time: 57.6 us; the launch traced here: 57.1 us
  Pallas kernels  54 us (94%)
  local copies, waits for them, and re-layouts  3.1 us (5%)
    pallas_call x1, Pallas kernels, on_device(): pl.pallas_call(functools.partial(kernel, n, doc_lengths.shape[0]), out_sh...  54 us
    unnamed x1, local copies, waits for them, and re-layouts  3.1 us

profile of v2, /device:TPU:5, one launch (start us, length us, event | category | flops | bytes accessed | tf_op | source)
XLA Modules:
  0.0 57.1 jit_solution(13743306965283750722)
XLA Ops:
  0.0 54.0 %attend_and_project.1 = bf16[128,8192]{1,0:T(8,128)(2,1)} custom-call(s32[8]{0:T(128)} %lengths.1, bf16[1,256,1024]{2,1,0:T(8,128)(2,1)} %q_hbm.1, bf16[1,256,128]{2,1,0:T(8,128)(2,1)} %k_ref.1, bf16[1,256,128]{2,1,0:T(8,128)(2,1)} %v_ref.1, bf16[1024,8192]{1,0:T(8,128)(2,1)} %w_hbm.1), custom_call_target="tpu_custom_call" | custom-call | flops 6576668672 | bytes 18874368 | tf_op jit(solution)/shard_map/attend_and_project/pallas_call | solution.py:350
  54.0 3.1 %copy.7 = bf16[128,8192]{1,0:T(8,128)(2,1)} copy(bf16[128,8192]{1,0:T(8,128)(2,1)} %attend_and_project.1) | data formatting | bytes 4194304

commit v3 on v1

--- a/solution.py
+++ b/solution.py
@@ -11,7 +11,7 @@
 MESH = pl.DeviceIdType.MESH
 NEG = -1e30
 FLOOR = -1e20
-COLUMNS = 512
+COLUMNS = 2048
 LAG = 2
 
 
@@ -22,10 +22,18 @@
     return z, rest // x, x
 
 
+def div(a, k):
+    return a >> (k.bit_length() - 1) if k & (k - 1) == 0 else a // k
+
+
+def mod(a, k):
+    return a & (k - 1) if k & (k - 1) == 0 else a % k
+
+
 def nearest(p, k, size):
     m = jnp.minimum(p, size - 1 - p)
-    half = (k + 1) // 2
-    near = jnp.where(k % 2 == 1, p + half, p - half)
+    half = div(k + 1, 2)
+    near = jnp.where(mod(k, 2) == 1, p + half, p - half)
     far = jnp.where(p < size - 1 - p, k, size - 1 - k)
     return jnp.where(k <= 2 * m, near, far)
 
@@ -66,7 +74,7 @@
     heads = width // hd
     me = lax.axis_index("ctx")
     core = lax.axis_index("kvh")
-    place = (me // (Y * X), (me // X) % Y, me % X)
+    place = (div(me, Y * X), mod(div(me, X), Y), mod(me, X))
     strides = (Y * X, X, 1)
 
     q_copy = pltpu.make_async_copy(q_hbm.at[0], q_in, local_sem.at[0])
@@ -108,7 +116,7 @@
 
     def tree(source, b):
         order = (0, 2, 1) if b == 0 else (0, 1, 2)
-        src = (source // (Y * X), (source // X) % Y, source % X)
+        src = (div(source, Y * X), mod(div(source, X), Y), mod(source, X))
         edges = []
         arrives = jnp.bool_(False)
         on_line = jnp.bool_(True)
@@ -224,13 +232,13 @@
         return index(
             (
                 nearest(place[0], kz, Z),
-                nearest(place[1], j // X, Y),
-                nearest(place[2], j % X, X),
+                nearest(place[1], div(j, X), Y),
+                nearest(place[2], mod(j, X), X),
             )
         )
 
     def visit(r, carry):
-        kz, j = r // plane, r % plane
+        kz, j = div(r, plane), mod(r, plane)
         source = source_at(kz, j)
 
         @pl.when((j == 0) & (kz + 1 < Z))

time: 53.5 us -> 50.5 us (0.944)
  Pallas kernels: 50.2 us -> 47.2 us
    pallas_call x1, Pallas kernels: 50.2 us -> 47.2 us  [on_device(): pl.pallas_call(functools.partial(kernel, n, doc_lengths.shape[0]), out_sh...]
where the time goes in v3:
time: 50.5 us; the launch traced here: 50.3 us
  Pallas kernels  47.2 us (93%)
  local copies, waits for them, and re-layouts  3.1 us (6%)
    pallas_call x1, Pallas kernels, on_device(): pl.pallas_call(functools.partial(kernel, n, doc_lengths.shape[0]), out_sh...  47.2 us
    unnamed x1, local copies, waits for them, and re-layouts  3.1 us

profile of v3, /device:TPU:5, one launch (start us, length us, event | category | flops | bytes accessed | tf_op | source)
XLA Modules:
  0.0 50.3 jit_solution(10556397995302813068)
XLA Ops:
  0.0 47.2 %attend_and_project.1 = bf16[128,8192]{1,0:T(8,128)(2,1)} custom-call(s32[8]{0:T(128)} %lengths.1, bf16[1,256,1024]{2,1,0:T(8,128)(2,1)} %q_hbm.1, bf16[1,256,128]{2,1,0:T(8,128)(2,1)} %k_ref.1, bf16[1,256,128]{2,1,0:T(8,128)(2,1)} %v_ref.1, bf16[1024,8192]{1,0:T(8,128)(2,1)} %w_hbm.1), custom_call_target="tpu_custom_call" | custom-call | flops 6576668672 | bytes 18874368 | tf_op jit(solution)/shard_map/attend_and_project/pallas_call | solution.py:360
  47.2 3.1 %copy.7 = bf16[128,8192]{1,0:T(8,128)(2,1)} copy(bf16[128,8192]{1,0:T(8,128)(2,1)} %attend_and_project.1) | data formatting | bytes 4194304

commit v4 on v3

--- a/solution.py
+++ b/solution.py
@@ -195,7 +195,7 @@
 
     factor = hd ** (-0.5) * math.log2(math.e)
     rows = lax.broadcasted_iota(jnp.int32, (block, block), 0)
-    group = 2 * hd if heads % 2 == 0 else hd
+    group = hd
 
     def absorb(qb, source, blocks):
         biases, keys, vals = [], [], []

time: 50.5 us -> 47.3 us (0.937)
  Pallas kernels: 47.2 us -> 44 us
    pallas_call x1, Pallas kernels: 47.2 us -> 44 us  [on_device(): pl.pallas_call(functools.partial(kernel, n, doc_lengths.shape[0]), out_sh...]
where the time goes in v4:
time: 47.3 us; the launch traced here: 47.1 us
  Pallas kernels  44 us (93%)
  local copies, waits for them, and re-layouts  3.1 us (7%)
    pallas_call x1, Pallas kernels, on_device(): pl.pallas_call(functools.partial(kernel, n, doc_lengths.shape[0]), out_sh...  44 us
    unnamed x1, local copies, waits for them, and re-layouts  3.1 us

profile of v4, /device:TPU:5, one launch (start us, length us, event | category | flops | bytes accessed | tf_op | source)
XLA Modules:
  0.0 47.1 jit_solution(15268206054464959067)
XLA Ops:
  0.0 44.0 %attend_and_project.1 = bf16[128,8192]{1,0:T(8,128)(2,1)} custom-call(s32[8]{0:T(128)} %lengths.1, bf16[1,256,1024]{2,1,0:T(8,128)(2,1)} %q_hbm.1, bf16[1,256,128]{2,1,0:T(8,128)(2,1)} %k_ref.1, bf16[1,256,128]{2,1,0:T(8,128)(2,1)} %v_ref.1, bf16[1024,8192]{1,0:T(8,128)(2,1)} %w_hbm.1), custom_call_target="tpu_custom_call" | custom-call | flops 6576668672 | bytes 18874368 | tf_op jit(solution)/shard_map/attend_and_project/pallas_call | solution.py:360
  44.0 3.1 %copy.7 = bf16[128,8192]{1,0:T(8,128)(2,1)} copy(bf16[128,8192]{1,0:T(8,128)(2,1)} %attend_and_project.1) | data formatting | bytes 4194304
